TPU v7x, 32 devices: a whole 2x2x4 slice. The times are simulated.
32 devices in a mesh: dp: 8 (over z, y), vocab: 4 (over x, core).
Axes of the slice: x: 2, y: 2, z: 4, core: 2. Of those that a mesh axis runs over, the one named last changes fastest.
Arguments:
- hidden_rows: bfloat16 [2048, 5120], P('dp'), may hold values from -300 to 300, as said below
- plan_lengths: int32 [8], replicated, may hold values from 1 to 256, 1024 in all
- shard_of_class: int32 [8], replicated, may hold values from 0 to 7, each once
- head_weight: bfloat16 [5120, 3072], P(None, 'vocab'), may hold values from -0.078125 to 0.078125
- teacher_logprobs: bfloat16 [1024, 3072], P('dp', 'vocab'), as said below
Outputs:
- row_grad: bfloat16 [2048, 5120], P('dp')
- row_kl: float32 [1024], P('dp')
Inputs may be any that keep to these rules, and one draw needn't show every extreme that they name: `plan_lengths`: the plan lengths sum to 1024 and the longest is exactly 256. `shard_of_class`: each shard is named once. `hidden_rows`: unused slots hold finite values. `teacher_logprobs`: each row is a log-softmax over the 3072 entries, rounded to bfloat16.
All inputs are finite; a program needn't handle non-finite values.
Results may differ from a plain program's by a relative error of at most 0.0046.
Values may be sent and summed in bfloat16 or wider, within the bound.
A program may use at most 64 MiB of HBM per device.

v0:
```python
import jax
import jax.numpy as jnp
from jax import lax
from jax.sharding import PartitionSpec as P

loss_scale = 64.0


def divergence(row_block, teacher_block, live_rows, weight):
    logits = jnp.dot(row_block, weight, preferred_element_type=jnp.float32)
    log_teacher = teacher_block.astype(jnp.float32)
    teacher_prob = jnp.exp(log_teacher)
    own_top = jnp.max(logits, axis=1)
    own_mass = jnp.sum(teacher_prob, axis=1)
    own_cross = jnp.sum(teacher_prob * (log_teacher - logits), axis=1)
    row_top = lax.pmax(own_top, "vocab")
    own_total = jnp.sum(jnp.exp(logits - row_top[:, None]), axis=1)
    exp_total, prob_total, cross_term = lax.psum((own_total, own_mass, own_cross), "vocab")
    log_total = row_top + jnp.log(exp_total)
    row_div = (cross_term + prob_total * log_total) * live_rows
    grad_logits = (
        loss_scale
        * (prob_total[:, None] * jnp.exp(logits - log_total[:, None]) - teacher_prob)
        * live_rows[:, None]
    ).astype(jnp.bfloat16)
    partial_grad = lax.dot_general(
        grad_logits, weight, (((1,), (1,)), ((), ())), preferred_element_type=jnp.float32
    )
    hidden_grad = lax.psum(partial_grad, "vocab").astype(jnp.bfloat16)
    return (hidden_grad, row_div)


def body(hidden_rows, plan_lengths, shard_of_class, head_weight, teacher_logprobs):
    shards = lax.axis_size("dp")
    myself = lax.axis_index("dp")
    source_slots = hidden_rows.shape[0]
    feature_width = hidden_rows.shape[1]
    slot_depth = source_slots // shards
    balanced = teacher_logprobs.shape[0]
    offsets = jnp.cumsum(plan_lengths) - plan_lengths
    classes = jnp.arange(shards, dtype=jnp.int32)
    inverse = jnp.sum(
        jnp.where(shard_of_class[None, :] == classes[:, None], classes[None, :], 0), axis=1
    )
    own_offset = offsets[myself]
    column_of = (inverse - own_offset) % shards
    shard_at = shard_of_class[(own_offset + classes) % shards]
    rank_rows = jnp.arange(slot_depth, dtype=jnp.int32)[:, None]
    recv_row = rank_rows * shards + ((inverse[myself] - offsets) % shards)[None, :]
    recv_live = recv_row < plan_lengths[None, :]
    recv_slot = jnp.where(recv_live, (offsets[None, :] + recv_row) // shards, balanced)
    safe_slot = jnp.minimum(recv_slot, balanced - 1).reshape(-1)
    outgoing = jnp.take(hidden_rows.reshape(slot_depth, shards, feature_width), column_of, axis=1)
    arriving = lax.all_to_all(outgoing, "dp", split_axis=1, concat_axis=1, tiled=True)
    flattened = arriving.reshape(slot_depth * shards, feature_width)
    live_rows = recv_live.reshape(-1).astype(jnp.float32)
    teacher_slots = jnp.take(teacher_logprobs, safe_slot, axis=0)
    returning, row_div = divergence(flattened, teacher_slots, live_rows, head_weight)
    row_kl = jnp.zeros((balanced,), jnp.float32).at[recv_slot.reshape(-1)].add(row_div, mode="drop")
    share_width = returning.shape[1]
    returned = lax.all_to_all(
        returning.reshape(slot_depth, shards, share_width),
        "dp",
        split_axis=1,
        concat_axis=1,
        tiled=True,
    )
    grad_share = jnp.take(returned, shard_at, axis=1).reshape(source_slots, share_width)
    return (grad_share, row_kl)


def solution(mesh):
    return jax.shard_map(
        body,
        mesh=mesh,
        in_specs=(P("dp", None), P(), P(), P(None, "vocab"), P("dp", "vocab")),
        out_specs=(P("dp", None), P("dp")),
        check_vma=False,
    )
```

profile of v0, /device:TPU:29, one launch (start us, length us, event | category | flops | bytes accessed | tf_op | source)
XLA Modules:
  0.0 275.9 jit_solution(15687510374739588956)
XLA Ops:
  0.6 0.0 copy-start
  0.6 0.8 select_reduce_fusion
  1.5 0.8 reduce-window.9
  2.3 0.6 dynamic_slice.6
  2.9 1.3 and_select_fusion.4
  4.2 0.6 dynamic_slice.7
  4.8 0.7 compare_and_fusion.1
  5.4 3.2 %copy.12 = bf16[32,8,5120]{2,0,1:T(8,128)(2,1)S(1)} copy(bf16[32,8,5120]{2,1,0:T(8,128)(2,1)} %bitcast.28) | data formatting | bytes 5242880 | tf_op jit(solution)/shard_map/reshape | solution.py:53
  8.6 2.2 gather_fusion.2
  10.8 3.5 %select_bitcast_fusion.1 = bf16[32,8,5120]{2,0,1:T(8,128)(2,1)} fusion(bf16[8,32,5120]{2,1,0:T(8,128)(2,1)} %gather_fusion.2, pred[8]{0:T(512)(128)(4,1)S(1)} %get-tuple-element.14), kind=kLoop, calls=%fused_computation.10 | loop fusion | flops 1310720 | bytes 5242888 | tf_op jit(solution)/shard_map/jit(_take)/select_n | solution.py:53
  14.4 0.0 copy-start.2
  14.4 5.6 %all-to-all-start = ((bf16[32,8,5120]{2,0,1:T(8,128)(2,1)}), bf16[32,8,5120]{2,0,1:T(8,128)(2,1)S(1)}, u32[]{:S(2)}, u32[]{:S(2)}) async-start(bf16[32,8,5120]{2,0,1:T(8,128)(2,1)} %select_bitcast_fusion.1), calls=%async_computation | async-start | bytes 5242880 | tf_op jit(solution)/shard_map/all_to_all | solution.py:54
  20.0 0.1 add_add_fusion
  20.0 0.1 add.179
  20.1 0.1 add.181
  20.2 0.0 copy-done.2
  20.2 0.1 add_compare_fusion
  20.3 0.1 lt.96
  20.4 0.1 lt.98
  20.5 0.0 copy-done
  20.6 1.2 gather_fusion
  21.8 56.0 %all-to-all-done = bf16[32,8,5120]{2,0,1:T(8,128)(2,1)S(1)} async-done(((bf16[32,8,5120]{2,0,1:T(8,128)(2,1)}), bf16[32,8,5120]{2,0,1:T(8,128)(2,1)S(1)}, u32[]{:S(2)}, u32[]{:S(2)}) %all-to-all-start) | async-done | bytes 2621472 | tf_op jit(solution)/shard_map/all_to_all | solution.py:54
  77.8 7.2 %fusion.22 = (f32[256]{0:T(256)S(1)}, f32[256,768]{1,0:T(8,128)}) fusion(bf16[5120,768]{1,0:T(8,128)(2,1)} %param.10, bf16[32,8,5120]{2,0,1:T(8,128)(2,1)S(1)} %all-to-all-done), kind=kOutput, calls=%fused_computation.72 | convolution fusion | flops 2013462272 | bytes 11273216 | tf_op jit(solution)/shard_map/dot_general | solution.py:10
  85.0 5.5 %pmax.7 = f32[256]{0:T(256)S(1)} all-reduce(f32[256]{0:T(256)S(1)} %get-tuple-element.16), channel_id=1, replica_groups=mesh['dp'=8,'vocab'=4] {'vocab'}, use_global_device_ids=true, to_apply=%region_5.7 | all-reduce | flops 256 | bytes 2048 | tf_op jit(solution)/shard_map/pmax | solution.py:16
  90.5 1.7 fusion.8
  92.2 6.9 %all-reduce.1 = (f32[256]{0:T(256)S(1)}, f32[256]{0:T(256)S(1)}) all-reduce(f32[256]{0:T(256)S(1)} %get-tuple-element.4, f32[256]{0:T(256)S(1)} %get-tuple-element.5), channel_id=1, replica_groups=mesh['dp'=8,'vocab'=4] {'vocab'}, use_global_device_ids=true, to_apply=%region_7.9 | all-reduce | flops 512 | bytes 4096 | tf_op jit(solution)/shard_map/psum | solution.py:18
  99.0 8.3 %fusion.9 = f32[256,5120]{1,0:T(8,128)} fusion(bf16[5120,768]{1,0:T(8,128)(2,1)} %param.10, f32[256,768]{1,0:T(8,128)} %get-tuple-element.17, f32[256]{0:T(256)S(1)} %broadcast_select_fusion.1, f32[256]{0:T(256)S(1)} %log_add_fusion, f32[256]{0:T(256)S(1)} %get-tuple-element.9, bf16[256,768]{1,0:T(8,128)(2,1)S(1)} %gather_fusion, ...), kind=kOutput, calls=%fused_computation.21 | convolution fusion | flops 2014642176 | bytes 14290176 | tf_op jit(solution)/shard_map/dot_general | solution.py:26
  107.3 94.8 %all-reduce.3 = (bf16[256,5120]{1,0:T(8,128)(2,1)S(1)}, f32[256]{0:T(256)S(1)}) all-reduce(f32[256,5120]{1,0:T(8,128)} %fusion.9, f32[256]{0:T(256)S(1)} %get-tuple-element.3), channel_id=1, replica_groups=mesh['dp'=8,'vocab'=4] {'vocab'}, use_global_device_ids=true, to_apply=%region_8.10 | all-reduce | flops 1310976 | bytes 7866368 | tf_op jit(solution)/shard_map/psum | solution.py:29
  202.1 2.9 %copy.14 = bf16[32,8,5120]{2,0,1:T(8,128)(2,1)} copy(bf16[32,8,5120]{2,1,0:T(8,128)(2,1)S(1)} %bitcast.30) | data formatting | bytes 5242880 | tf_op jit(solution)/shard_map/reshape | solution.py:62
  205.0 0.0 copy-start.1
  205.0 5.9 %all-to-all-start.1 = ((bf16[32,8,5120]{2,0,1:T(8,128)(2,1)}), bf16[32,8,5120]{2,0,1:T(8,128)(2,1)S(1)}, u32[]{:S(2)}, u32[]{:S(2)}) async-start(bf16[32,8,5120]{2,0,1:T(8,128)(2,1)} %copy.14), calls=%async_computation.1 | async-start | bytes 5242880 | tf_op jit(solution)/shard_map/all_to_all | solution.py:61
  210.9 0.7 fusion.18
  211.6 0.0 copy-done.1
  211.6 0.6 gather_fusion.1
  212.3 2.8 %scatter_custom_fusion = f32[128]{0:T(128)} fusion(s32[256]{0:T(256)S(1)} %bitcast.33, f32[256]{0:T(256)S(1)} %add_select_fusion, f32[]{:T(128)} %constant.86.clone.1), kind=kCustom, calls=%fused_computation.70 | custom fusion | flops 256 | bytes 516 | tf_op jit(solution)/shard_map/scatter-add | solution.py:59
  215.1 53.6 %all-to-all-done.1 = bf16[32,8,5120]{2,0,1:T(8,128)(2,1)S(1)} async-done(((bf16[32,8,5120]{2,0,1:T(8,128)(2,1)}), bf16[32,8,5120]{2,0,1:T(8,128)(2,1)S(1)}, u32[]{:S(2)}, u32[]{:S(2)}) %all-to-all-start.1) | async-done | bytes 2621472 | tf_op jit(solution)/shard_map/all_to_all | solution.py:61
  268.8 2.2 gather_fusion.3
  271.0 2.1 select_bitcast_fusion
  273.0 2.9 %copy.23 = bf16[32,8,5120]{2,1,0:T(8,128)(2,1)} copy(bf16[32,8,5120]{2,0,1:T(8,128)(2,1)S(1)} %select_bitcast_fusion) | data formatting | bytes 5242880 | tf_op jit(solution)/shard_map/jit(_take)/select_n | solution.py:68
  (13 shorter events, 0.1 us)
Async XLA Ops:
  0.6 19.9 %copy-start = (bf16[128,768]{1,0:T(8,128)(2,1)S(1)}, bf16[128,768]{1,0:T(8,128)(2,1)}, u32[]{:S(2)}) copy-start(bf16[128,768]{1,0:T(8,128)(2,1)} %param.11) | copy-start | bytes 589828
  14.4 5.8 %copy-start.2 = (s32[8]{0:T(128)S(1)}, s32[8]{0:T(128)}, u32[]{:S(2)}) copy-start(s32[8]{0:T(128)} %param.8) | copy-start | bytes 100
  14.4 63.4 %all-to-all-start = ((bf16[32,8,5120]{2,0,1:T(8,128)(2,1)}), bf16[32,8,5120]{2,0,1:T(8,128)(2,1)S(1)}, u32[]{:S(2)}, u32[]{:S(2)}) async-start(bf16[32,8,5120]{2,0,1:T(8,128)(2,1)} %select_bitcast_fusion.1), calls=%async_computation | async-start | bytes 5242880 | tf_op jit(solution)/shard_map/all_to_all | solution.py:54
  205.0 6.6 %copy-start.1 = (s32[8]{0:T(128)S(1)}, s32[8]{0:T(128)}, u32[]{:S(2)}) copy-start(s32[8]{0:T(128)} %param.9) | copy-start | bytes 100
  205.0 63.7 %all-to-all-start.1 = ((bf16[32,8,5120]{2,0,1:T(8,128)(2,1)}), bf16[32,8,5120]{2,0,1:T(8,128)(2,1)S(1)}, u32[]{:S(2)}, u32[]{:S(2)}) async-start(bf16[32,8,5120]{2,0,1:T(8,128)(2,1)} %copy.14), calls=%async_computation.1 | async-start | bytes 5242880 | tf_op jit(solution)/shard_map/all_to_all | solution.py:61
where the time goes:
time: 280 us; the launch traced here: 276 us
  waiting for transfers between devices  110 us (39%)
  blocking collectives  107 us (38%)
  local copies, waits for them, and re-layouts  16.8 us (6%)
  matrix products  15.5 us (6%)
  other arithmetic  14.6 us (5%)
  starting transfers between devices  11.4 us (4%)
    psum x1, blocking collectives, divergence(): hidden_grad = lax.psum(partial_grad, 'vocab').astype(jnp.bfloat16)  94.8 us
    all_to_all x1, waiting for transfers between devices, body(): lax.all_to_all(outgoing, 'dp', split_axis=1, concat_axis=1, tiled=True)  56 us
    all_to_all x1, waiting for transfers between devices, body(): lax.all_to_all(returning.reshape(slot_depth, shards, share_width), 'dp',...  53.6 us
    dot_general x1, matrix products, divergence(): lax.dot_general(grad_logits, weight, (((1,), (1,)), ((), ())), preferred_...  8.26 us
    dot_general x1, matrix products, divergence(): logits = jnp.dot(row_block, weight, preferred_element_type=jnp.float32)  7.21 us
    psum x1, blocking collectives, divergence(): lax.psum((own_total, own_mass, own_cross), 'vocab')  6.87 us
    all_to_all x1, starting transfers between devices, body(): lax.all_to_all(returning.reshape(slot_depth, shards, share_width), 'dp',...  5.88 us
  transfers between devices with their start and end apart: 2, of which 2 were waited for; matrix products, arithmetic and copies ran while one was open for 2% of the time, Pallas kernels for 0%

commit v1 on v0

v1 whole, which is shorter than its diff:
```python
import functools

import jax
import jax.numpy as jnp
from jax import lax
from jax.experimental import pallas as pl
from jax.experimental.pallas import tpu as pltpu
from jax.sharding import PartitionSpec as P

loss_scale = 64.0
MESH = pl.DeviceIdType.MESH
GROUPS = 2
KBLK = 512
CBLK = 512


def kernel(
    n,
    nv,
    len_ref,
    soc_ref,
    teach_ref,
    hid_hbm,
    w_hbm,
    out_hbm,
    kl_ref,
    w_v,
    h_v,
    z_v,
    q_v,
    g_v,
    tout,
    tin,
    st,
    klb,
    sib_out,
    sib_in,
    xs,
    xr,
    fin,
    w_sem,
    h_sem,
    ts_sem,
    tr_sem,
    tl_sem,
    ss_sem,
    sr_sem,
    ks_sem,
    kr_sem,
    bs_sem,
    br_sem,
    xs_sem,
    xr_sem,
    fs_sem,
    fr_sem,
    fl_sem,
):
    me = lax.axis_index("dp")
    v = lax.axis_index("vocab")
    core = lax.rem(v, 2)
    sib = v + 1 - 2 * core
    across = lax.rem(v + 2, 4)
    slots, feat = hid_hbm.shape
    bal, vloc = teach_ref.shape
    steps = feat // KBLK
    rows = slots // GROUPS
    half = feat // 2
    chunks = half // CBLK
    per = rows // n
    dep = tin.shape[2]
    shift = n.bit_length() - 1

    barrier = pltpu.get_barrier_semaphore()
    for k in range(1, n):
        pl.semaphore_signal(barrier, 1, device_id=(lax.rem(me + k, n), v), device_id_type=MESH)
    for k in range(1, nv):
        pl.semaphore_signal(barrier, 1, device_id=(me, lax.rem(v + k, nv)), device_id_type=MESH)

    def w_load(k):
        return pltpu.make_async_copy(
            w_hbm.at[pl.ds(pl.multiple_of(k * KBLK, KBLK), KBLK), :],
            w_v.at[pl.ds(pl.multiple_of(k * KBLK, KBLK), KBLK), :],
            w_sem.at[k],
        )

    def h_load(k):
        return pltpu.make_async_copy(
            hid_hbm.at[:, pl.ds(pl.multiple_of(k * KBLK, KBLK), KBLK)], h_v.at[k], h_sem.at[k]
        )

    @pl.loop(0, steps)
    def _(k):
        w_load(k).start()
        h_load(k).start()

    lens, offs, run = [], [], jnp.int32(0)
    for s in range(n):
        ln = len_ref[s]
        lens.append(ln)
        offs.append(run)
        run = run + ln
    zero = jnp.int32(0)
    inv_me, off_me, len_me = zero, zero, zero
    for s in range(n):
        inv_me = inv_me + jnp.where(soc_ref[s] == me, jnp.int32(s), zero)
        off_me = off_me + jnp.where(me == s, offs[s], zero)
        len_me = len_me + jnp.where(me == s, lens[s], zero)

    for g in range(GROUPS):
        for s in range(n):
            b0 = lax.shift_right_logical(offs[s] + ((inv_me - offs[s]) & (n - 1)), shift)
            first = b0 + g * per
            r = lax.broadcasted_iota(jnp.int32, (dep, bal), 0)
            b = lax.broadcasted_iota(jnp.int32, (dep, bal), 1)
            hot = jnp.where(b == r + first, 1.0, 0.0).astype(jnp.bfloat16)
            tout[g, s] = jnp.dot(
                hot, teach_ref[...], preferred_element_type=jnp.float32
            ).astype(jnp.bfloat16)

    def t_send(g, to):
        return pltpu.make_async_remote_copy(
            src_ref=tout.at[g, to],
            dst_ref=tin.at[g, me],
            send_sem=ts_sem.at[g, to],
            recv_sem=tr_sem.at[g, me],
            device_id=(to, v),
            device_id_type=MESH,
        )

    def t_recv(g, frm):
        return pltpu.make_async_remote_copy(
            src_ref=tout.at[g, frm],
            dst_ref=tin.at[g, frm],
            send_sem=ts_sem.at[g, frm],
            recv_sem=tr_sem.at[g, frm],
            device_id=(frm, v),
            device_id_type=MESH,
        )

    def t_own(g):
        return pltpu.make_async_copy(tout.at[g, me], tin.at[g, me], tl_sem.at[g])

    pl.semaphore_wait(barrier, n - 1 + nv - 1)
    for g in range(GROUPS):
        t_own(g).start()

        @pl.loop(1, n)
        def _(k):
            t_send(g, lax.rem(me + k, n)).start()

    z_v[...] = jnp.zeros_like(z_v)

    @pl.loop(0, steps)
    def _(k):
        w_load(k).wait()
        h_load(k).wait()
        z_v[...] += jnp.dot(
            h_v[k],
            w_v[pl.ds(pl.multiple_of(k * KBLK, KBLK), KBLK), :],
            preferred_element_type=jnp.float32,
        )

    def s_copy(g, frm, to):
        return pltpu.make_async_remote_copy(
            src_ref=st.at[g, frm],
            dst_ref=st.at[g, frm],
            send_sem=ss_sem.at[g, to],
            recv_sem=sr_sem.at[g, frm],
            device_id=(me, to),
            device_id_type=MESH,
        )

    def b_copy(g, j):
        return pltpu.make_async_remote_copy(
            src_ref=sib_out.at[g, j],
            dst_ref=sib_in.at[g, j],
            send_sem=bs_sem.at[g, j],
            recv_sem=br_sem.at[g, j],
            device_id=(me, sib),
            device_id_type=MESH,
        )

    def x_copy(g, j):
        return pltpu.make_async_remote_copy(
            src_ref=xs.at[g, j],
            dst_ref=xr.at[g, j],
            send_sem=xs_sem.at[g, j],
            recv_sem=xr_sem.at[g, j],
            device_id=(me, across),
            device_id_type=MESH,
        )

    def place(g, owner, j):
        col = pl.multiple_of(owner * half + j * CBLK, 128)
        return out_hbm.at[pl.ds(g * rows, rows), pl.ds(col, CBLK)]

    def f_send(g, j):
        return pltpu.make_async_remote_copy(
            src_ref=fin.at[g, j],
            dst_ref=place(g, core, j),
            send_sem=fs_sem.at[g, j],
            recv_sem=fr_sem.at[g, j],
            device_id=(me, sib),
            device_id_type=MESH,
        )

    def f_recv(g, j):
        return pltpu.make_async_remote_copy(
            src_ref=fin.at[g, j],
            dst_ref=place(g, 1 - core, j),
            send_sem=fs_sem.at[g, j],
            recv_sem=fr_sem.at[g, j],
            device_id=(me, sib),
            device_id_type=MESH,
        )

    def f_own(g, j):
        return pltpu.make_async_copy(fin.at[g, j], place(g, core, j), fl_sem.at[g, j])

    def w_rows(owner, j):
        return w_v[pl.ds(pl.multiple_of(owner * half + j * CBLK, CBLK), CBLK), :]

    def back(g, owner, j):
        return lax.dot_general(
            g_v[pl.ds(g * rows, rows), :],
            w_rows(owner, j),
            (((1,), (1,)), ((), ())),
            preferred_element_type=jnp.float32,
        )

    for g in range(GROUPS):
        span = pl.ds(g * rows, rows)
        slot = lax.broadcasted_iota(jnp.int32, (rows, 1), 0) + g * rows
        live = slot < len_me
        cls = (off_me + slot) & (n - 1)
        owner = jnp.zeros((rows, 1), jnp.int32)
        for c in range(n):
            owner = owner + jnp.where(cls == c, soc_ref[c], zero)
        rank = lax.shift_right_logical(slot, shift) - g * per
        pick = owner * dep + rank
        lane = lax.broadcasted_iota(jnp.int32, (rows, n * dep), 1)
        hot = jnp.where(lane == pick, 1.0, 0.0).astype(jnp.bfloat16)

        t_own(g).wait()

        @pl.loop(1, n)
        def _(k):
            t_recv(g, lax.rem(me + k, n)).wait_recv()

        t = jnp.dot(
            hot, tin[g].reshape(n * dep, vloc), preferred_element_type=jnp.float32
        )
        z = jnp.where(live, z_v[span, :], 0.0)
        q = jnp.exp(t)
        q_v[span, :] = q
        top = jnp.max(z, axis=1, keepdims=True)
        total = jnp.sum(jnp.exp(z - top), axis=1, keepdims=True)
        mass = jnp.sum(q, axis=1, keepdims=True)
        cross = jnp.sum(q * (t - z), axis=1, keepdims=True)
        col = lax.broadcasted_iota(jnp.int32, (rows, 128), 1)
        packed = jnp.where(
            col == 0, top, jnp.where(col == 1, total, jnp.where(col == 2, mass, cross))
        )
        st[g, v] = packed.T[:8, :]

        @pl.loop(1, nv)
        def _(k):
            s_copy(g, v, lax.rem(v + k, nv)).start()

        @pl.loop(1, nv)
        def _(k):
            frm = lax.rem(v + k, nv)
            s_copy(g, frm, frm).wait_recv()

        peak = st[g, 0, 0:1, :]
        for u in range(1, nv):
            peak = jnp.maximum(peak, st[g, u, 0:1, :])
        sums = jnp.zeros_like(peak)
        masses = jnp.zeros_like(peak)
        crosses = jnp.zeros_like(peak)
        for u in range(nv):
            sums = sums + st[g, u, 1:2, :] * jnp.exp(st[g, u, 0:1, :] - peak)
            masses = masses + st[g, u, 2:3, :]
            crosses = crosses + st[g, u, 3:4, :]
        lse = peak + jnp.log(sums)
        klb[me, :, pl.ds(g * rows, rows)] = jnp.broadcast_to(crosses + masses * lse, (8, rows))
        sub = lax.broadcasted_iota(jnp.int32, (128, rows), 0)
        back_cols = jnp.where(sub == 0, lse, masses).T
        lse_c = back_cols[:, 0:1]
        mass_c = back_cols[:, 1:2]
        z = jnp.where(live, z_v[span, :], 0.0)
        grad = loss_scale * (mass_c * jnp.exp(z - lse_c) - q_v[span, :])
        g_v[span, :] = jnp.where(live, grad, 0.0).astype(jnp.bfloat16)

        @pl.loop(0, chunks)
        def _(j):
            sib_out[g, j] = back(g, 1 - core, j)
            b_copy(g, j).start()

        @pl.loop(0, chunks)
        def _(j):
            mine = back(g, core, j)
            b_copy(g, j).wait_recv()
            xs[g, j] = (mine + sib_in[g, j]).astype(jnp.bfloat16)
            x_copy(g, j).start()

    def k_copy(frm, to):
        return pltpu.make_async_remote_copy(
            src_ref=klb.at[frm],
            dst_ref=klb.at[frm],
            send_sem=ks_sem.at[to],
            recv_sem=kr_sem.at[frm],
            device_id=(to, v),
            device_id_type=MESH,
        )

    @pl.loop(1, n)
    def _(k):
        k_copy(me, lax.rem(me + k, n)).start()

    @pl.loop(1, n)
    def _(k):
        frm = lax.rem(me + k, n)
        k_copy(frm, frm).wait_recv()

    want = lax.broadcasted_iota(jnp.int32, (bal, slots), 0) * n + inv_me
    inner = lax.broadcasted_iota(jnp.int32, (bal, slots), 1)
    acc = jnp.zeros((bal, slots), jnp.float32)
    for s in range(n):
        hit = (want - offs[s] == inner) & (inner < lens[s])
        acc = jnp.where(hit, klb[s, 0:1, :], acc)
    kl_col = jnp.sum(acc, axis=1, keepdims=True)
    diag = lax.broadcasted_iota(jnp.int32, (bal, bal), 0) == lax.broadcasted_iota(
        jnp.int32, (bal, bal), 1
    )
    kl_ref[...] = jnp.sum(jnp.where(diag, kl_col, 0.0), axis=0, keepdims=True)

    for g in range(GROUPS):

        @pl.loop(0, chunks)
        def _(j):
            x_copy(g, j).wait_recv()
            fin[g, j] = (xs[g, j].astype(jnp.float32) + xr[g, j].astype(jnp.float32)).astype(
                jnp.bfloat16
            )
            f_send(g, j).start()
            f_own(g, j).start()

    for g in range(GROUPS):

        @pl.loop(1, n)
        def _(k):
            t_send(g, lax.rem(me + k, n)).wait_send()

        @pl.loop(1, nv)
        def _(k):
            s_copy(g, v, lax.rem(v + k, nv)).wait_send()

        @pl.loop(0, chunks)
        def _(j):
            b_copy(g, j).wait_send()
            x_copy(g, j).wait_send()
            f_send(g, j).wait_send()
            f_own(g, j).wait()
            f_recv(g, j).wait_recv()

    @pl.loop(1, n)
    def _(k):
        k_copy(me, lax.rem(me + k, n)).wait_send()


def body(hidden_rows, plan_lengths, shard_of_class, head_weight, teacher_logprobs):
    n = lax.axis_size("dp")
    nv = lax.axis_size("vocab")
    slots, feat = hidden_rows.shape
    bal, vloc = teacher_logprobs.shape
    steps = feat // KBLK
    rows = slots // GROUPS
    chunks = feat // 2 // CBLK
    dep = max(16, rows // n)
    dma = pltpu.SemaphoreType.DMA
    bf, f32 = jnp.bfloat16, jnp.float32
    flops = 4 * slots * feat * vloc
    row_grad, row_kl = pl.pallas_call(
        functools.partial(kernel, n, nv),
        out_shape=(
            jax.ShapeDtypeStruct((slots, feat), bf),
            jax.ShapeDtypeStruct((1, bal), f32),
        ),
        in_specs=[
            pl.BlockSpec(memory_space=pltpu.SMEM),
            pl.BlockSpec(memory_space=pltpu.SMEM),
            pl.BlockSpec(memory_space=pltpu.VMEM),
            pl.BlockSpec(memory_space=pl.ANY),
            pl.BlockSpec(memory_space=pl.ANY),
        ],
        out_specs=(
            pl.BlockSpec(memory_space=pl.ANY),
            pl.BlockSpec(memory_space=pltpu.VMEM),
        ),
        scratch_shapes=[
            pltpu.VMEM((feat, vloc), bf),
            pltpu.VMEM((steps, slots, KBLK), bf),
            pltpu.VMEM((slots, vloc), f32),
            pltpu.VMEM((slots, vloc), f32),
            pltpu.VMEM((slots, vloc), bf),
            pltpu.VMEM((GROUPS, n, dep, vloc), bf),
            pltpu.VMEM((GROUPS, n, dep, vloc), bf),
            pltpu.VMEM((GROUPS, nv, 8, rows), f32),
            pltpu.VMEM((n, 8, slots), f32),
            pltpu.VMEM((GROUPS, chunks, rows, CBLK), f32),
            pltpu.VMEM((GROUPS, chunks, rows, CBLK), f32),
            pltpu.VMEM((GROUPS, chunks, rows, CBLK), bf),
            pltpu.VMEM((GROUPS, chunks, rows, CBLK), bf),
            pltpu.VMEM((GROUPS, chunks, rows, CBLK), bf),
            dma((steps,)),
            dma((steps,)),
            dma((GROUPS, n)),
            dma((GROUPS, n)),
            dma((GROUPS,)),
            dma((GROUPS, nv)),
            dma((GROUPS, nv)),
            dma((n,)),
            dma((n,)),
            dma((GROUPS, chunks)),
            dma((GROUPS, chunks)),
            dma((GROUPS, chunks)),
            dma((GROUPS, chunks)),
            dma((GROUPS, chunks)),
            dma((GROUPS, chunks)),
            dma((GROUPS, chunks)),
        ],
        compiler_params=pltpu.CompilerParams(
            collective_id=0, has_side_effects=True, vmem_limit_bytes=50 * 1024 * 1024
        ),
        cost_estimate=pl.CostEstimate(
            flops=flops, bytes_accessed=2 * feat * (vloc + 2 * slots), transcendentals=3 * slots * vloc
        ),
        name="plan_loss",
    )(plan_lengths, shard_of_class, teacher_logprobs, hidden_rows, head_weight)
    return row_grad, row_kl.reshape(bal)


def solution(mesh):
    return jax.shard_map(
        body,
        mesh=mesh,
        in_specs=(P("dp", None), P(), P(), P(None, "vocab"), P("dp", "vocab")),
        out_specs=(P("dp", None), P("dp")),
        check_vma=False,
    )
```

time: 280 us -> 61.2 us (0.22); the launches traced: 276 us -> 61 us
  waiting for transfers between devices: 110 us -> 0 us
  blocking collectives: 107 us -> 0 us
  Pallas kernels: 0 us -> 56.1 us
  matrix products: 15.5 us -> 0 us
  other arithmetic: 14.6 us -> 0 us
  local copies, waits for them, and re-layouts: 16.8 us -> 4.23 us
  starting transfers between devices: 11.4 us -> 0 us
    all_to_all x2 -> x0, waiting for transfers between devices: 110 us -> none  [the longest x1 56 us: body(): lax.all_to_all(outgoing, 'dp', split_axis=1, concat_axis=1, tiled=True)]
    psum x2 -> x0, blocking collectives: 102 us -> none  [the longest x1 94.8 us: divergence(): hidden_grad = lax.psum(partial_grad, 'vocab').astype(jnp.bfloat16)]
    pallas_call x0 -> x1, Pallas kernels: none -> 56.1 us  [body(): pl.pallas_call(functools.partial(kernel, n, nv), out_shape=(jax.ShapeDtyp...]
    dot_general x2 -> x0, matrix products: 15.5 us -> none  [the longest x1 8.26 us: divergence(): lax.dot_general(grad_logits, weight, (((1,), (1,)), ((), ())), preferred_...]
    all_to_all x2 -> x0, starting transfers between devices: 11.4 us -> none  [the longest x1 5.88 us: body(): lax.all_to_all(returning.reshape(slot_depth, shards, share_width), 'dp',...]
    select_n x7 -> x0, other arithmetic: 7.59 us -> none  [the longest x1 3.55 us: body(): jnp.take(hidden_rows.reshape(slot_depth, shards, feature_width), column_o...]
    gather x4 -> x0, local copies, waits for them, and re-layouts: 6.24 us -> none  [the longest x1 2.21 us: body(): jnp.take(hidden_rows.reshape(slot_depth, shards, feature_width), column_o...]
    reshape x2 -> x0, local copies, waits for them, and re-layouts: 6.11 us -> none  [the longest x1 3.18 us: body(): hidden_rows.reshape(slot_depth, shards, feature_width)]
  transfers between devices with their start and end apart: 2 -> 0, of which waited for: 2 -> 0; matrix products, arithmetic and copies ran while one was open for 2% -> 0% of each run, Pallas kernels for 0% -> 0%
where the time goes in v1:
time: 61.2 us; the launch traced here: 61 us
  Pallas kernels  56.1 us (92%)
  local copies, waits for them, and re-layouts  4.23 us (7%)
  between operations  0.65 us (1%)
    pallas_call x1, Pallas kernels, body(): pl.pallas_call(functools.partial(kernel, n, nv), out_shape=(jax.ShapeDtyp...  56.1 us
    unnamed x8, local copies, waits for them, and re-layouts  4.23 us

profile of v1, /device:TPU:29, one launch (start us, length us, event | category | flops | bytes accessed | tf_op | source)
XLA Modules:
  0.0 61.0 jit_solution(12929487237424332472)
XLA Ops:
  0.6 0.0 copy-start
  0.6 0.9 %copy-done = bf16[128,768]{1,0:T(8,128)(2,1)S(1)} copy-done((bf16[128,768]{1,0:T(8,128)(2,1)S(1)}, bf16[128,768]{1,0:T(8,128)(2,1)}, u32[]{:S(2)}) %copy-start) | copy-done | bytes 196632
  1.6 0.0 copy-start.1
  1.6 0.7 %copy-done.1 = s32[8]{0:T(128)S(1)} copy-done((s32[8]{0:T(128)S(1)}, s32[8]{0:T(128)}, u32[]{:S(2)}) %copy-start.1) | copy-done | bytes 56
  2.2 0.0 copy-start.2
  2.2 0.7 %copy-done.2 = s32[8]{0:T(128)S(1)} copy-done((s32[8]{0:T(128)S(1)}, s32[8]{0:T(128)}, u32[]{:S(2)}) %copy-start.2) | copy-done | bytes 56
  2.9 56.1 %plan_loss.1 = (bf16[256,5120]{1,0:T(8,128)(2,1)S(1)}, f32[1,128]{1,0:T(1,128)S(1)}) custom-call(s32[8]{0:T(128)S(1)} %copy-done.1, s32[8]{0:T(128)S(1)} %copy-done.2, bf16[128,768]{1,0:T(8,128)(2,1)S(1)} %copy-done, bf16[256,5120]{1,0:T(8,128)(2,1)} %hid_hbm.1, bf16[5120,768]{1,0:T(8,128)(2,1)} %w_hbm.1), custom_call_target="tpu_custom_call" | custom-call | flops 4026531840 | bytes 13107200 | tf_op jit(solution)/shard_map/plan_loss/pallas_call | solution.py:384
  59.0 1.5 %copy.9 = bf16[256,5120]{1,0:T(8,128)(2,1)} copy(bf16[256,5120]{1,0:T(8,128)(2,1)S(1)} %get-tuple-element.8) | data formatting | bytes 5242880
  60.5 0.5 copy.10
Async XLA Ops:
  0.6 0.9 %copy-start = (bf16[128,768]{1,0:T(8,128)(2,1)S(1)}, bf16[128,768]{1,0:T(8,128)(2,1)}, u32[]{:S(2)}) copy-start(bf16[128,768]{1,0:T(8,128)(2,1)} %teach_ref.1) | copy-start | bytes 589828
  1.6 0.7 %copy-start.1 = (s32[8]{0:T(128)S(1)}, s32[8]{0:T(128)}, u32[]{:S(2)}) copy-start(s32[8]{0:T(128)} %len_ref.1) | copy-start | bytes 100
  2.2 0.7 %copy-start.2 = (s32[8]{0:T(128)S(1)}, s32[8]{0:T(128)}, u32[]{:S(2)}) copy-start(s32[8]{0:T(128)} %soc_ref.1) | copy-start | bytes 100

commit v2 on v1

--- a/solution.py
+++ b/solution.py
@@ -17,14 +17,18 @@
 def kernel(
     n,
     nv,
-    len_ref,
-    soc_ref,
-    teach_ref,
+    len_hbm,
+    soc_hbm,
+    teach_hbm,
     hid_hbm,
     w_hbm,
     out_hbm,
     kl_ref,
+    len_ref,
+    soc_ref,
+    teach_ref,
     w_v,
+    w_sib,
     h_v,
     z_v,
     q_v,
@@ -33,11 +37,11 @@
     tin,
     st,
     klb,
-    sib_out,
-    sib_in,
+    g_sib,
     xs,
     xr,
     fin,
+    i_sem,
     w_sem,
     h_sem,
     ts_sem,
@@ -47,8 +51,10 @@
     sr_sem,
     ks_sem,
     kr_sem,
-    bs_sem,
-    br_sem,
+    ws_sem,
+    wr_sem,
+    gs_sem,
+    gr_sem,
     xs_sem,
     xr_sem,
     fs_sem,
@@ -58,6 +64,7 @@
     me = lax.axis_index("dp")
     v = lax.axis_index("vocab")
     core = lax.rem(v, 2)
+    sib_core = 1 - core
     sib = v + 1 - 2 * core
     across = lax.rem(v + 2, 4)
     slots, feat = hid_hbm.shape
@@ -70,6 +77,14 @@
     dep = tin.shape[2]
     shift = n.bit_length() - 1
 
+    small = [
+        pltpu.make_async_copy(len_hbm, len_ref, i_sem.at[0]),
+        pltpu.make_async_copy(soc_hbm, soc_ref, i_sem.at[1]),
+        pltpu.make_async_copy(teach_hbm, teach_ref, i_sem.at[2]),
+    ]
+    for copy in small:
+        copy.start()
+
     barrier = pltpu.get_barrier_semaphore()
     for k in range(1, n):
         pl.semaphore_signal(barrier, 1, device_id=(lax.rem(me + k, n), v), device_id_type=MESH)
@@ -92,6 +107,9 @@
     def _(k):
         w_load(k).start()
         h_load(k).start()
+
+    for copy in small:
+        copy.wait()
 
     lens, offs, run = [], [], jnp.int32(0)
     for s in range(n):
@@ -140,8 +158,25 @@
     def t_own(g):
         return pltpu.make_async_copy(tout.at[g, me], tin.at[g, me], tl_sem.at[g])
 
+    def w_push(j):
+        row = pl.multiple_of(sib_core * half + j * CBLK, CBLK)
+        return pltpu.make_async_remote_copy(
+            src_ref=w_hbm.at[pl.ds(row, CBLK), :],
+            dst_ref=w_sib.at[j],
+            send_sem=ws_sem.at[j],
+            recv_sem=wr_sem.at[j],
+            device_id=(me, sib),
+            device_id_type=MESH,
+        )
+
     pl.semaphore_wait(barrier, n - 1 + nv - 1)
     for g in range(GROUPS):
+        if g == 1:
+
+            @pl.loop(0, chunks)
+            def _(j):
+                w_push(j).start()
+
         t_own(g).start()
 
         @pl.loop(1, n)
@@ -170,12 +205,12 @@
             device_id_type=MESH,
         )
 
-    def b_copy(g, j):
-        return pltpu.make_async_remote_copy(
-            src_ref=sib_out.at[g, j],
-            dst_ref=sib_in.at[g, j],
-            send_sem=bs_sem.at[g, j],
-            recv_sem=br_sem.at[g, j],
+    def g_copy(g):
+        return pltpu.make_async_remote_copy(
+            src_ref=g_v.at[pl.ds(g * rows, rows), :],
+            dst_ref=g_sib.at[pl.ds(g * rows, rows), :],
+            send_sem=gs_sem.at[g],
+            recv_sem=gr_sem.at[g],
             device_id=(me, sib),
             device_id_type=MESH,
         )
@@ -217,15 +252,9 @@
     def f_own(g, j):
         return pltpu.make_async_copy(fin.at[g, j], place(g, core, j), fl_sem.at[g, j])
 
-    def w_rows(owner, j):
-        return w_v[pl.ds(pl.multiple_of(owner * half + j * CBLK, CBLK), CBLK), :]
-
-    def back(g, owner, j):
+    def back(grad, weight):
         return lax.dot_general(
-            g_v[pl.ds(g * rows, rows), :],
-            w_rows(owner, j),
-            (((1,), (1,)), ((), ())),
-            preferred_element_type=jnp.float32,
+            grad, weight, (((1,), (1,)), ((), ())), preferred_element_type=jnp.float32
         )
 
     for g in range(GROUPS):
@@ -292,16 +321,16 @@
         grad = loss_scale * (mass_c * jnp.exp(z - lse_c) - q_v[span, :])
         g_v[span, :] = jnp.where(live, grad, 0.0).astype(jnp.bfloat16)
 
+        g_copy(g).start()
+        g_copy(g).wait_recv()
+
         @pl.loop(0, chunks)
         def _(j):
-            sib_out[g, j] = back(g, 1 - core, j)
-            b_copy(g, j).start()
-
-        @pl.loop(0, chunks)
-        def _(j):
-            mine = back(g, core, j)
-            b_copy(g, j).wait_recv()
-            xs[g, j] = (mine + sib_in[g, j]).astype(jnp.bfloat16)
+            if g == 0:
+                w_push(j).wait_recv()
+            own = w_v[pl.ds(pl.multiple_of(core * half + j * CBLK, CBLK), CBLK), :]
+            mine = back(g_v[span, :], own) + back(g_sib[span, :], w_sib[j])
+            xs[g, j] = mine.astype(jnp.bfloat16)
             x_copy(g, j).start()
 
     def k_copy(frm, to):
@@ -352,13 +381,16 @@
         def _(k):
             t_send(g, lax.rem(me + k, n)).wait_send()
 
+        g_copy(g).wait_send()
+
         @pl.loop(1, nv)
         def _(k):
             s_copy(g, v, lax.rem(v + k, nv)).wait_send()
 
         @pl.loop(0, chunks)
         def _(j):
-            b_copy(g, j).wait_send()
+            if g == 0:
+                w_push(j).wait_send()
             x_copy(g, j).wait_send()
             f_send(g, j).wait_send()
             f_own(g, j).wait()
@@ -388,18 +420,22 @@
             jax.ShapeDtypeStruct((1, bal), f32),
         ),
         in_specs=[
-            pl.BlockSpec(memory_space=pltpu.SMEM),
-            pl.BlockSpec(memory_space=pltpu.SMEM),
-            pl.BlockSpec(memory_space=pltpu.VMEM),
-            pl.BlockSpec(memory_space=pl.ANY),
-            pl.BlockSpec(memory_space=pl.ANY),
+            pl.BlockSpec(memory_space=pltpu.HBM),
+            pl.BlockSpec(memory_space=pltpu.HBM),
+            pl.BlockSpec(memory_space=pltpu.HBM),
+            pl.BlockSpec(memory_space=pltpu.HBM),
+            pl.BlockSpec(memory_space=pltpu.HBM),
         ],
         out_specs=(
             pl.BlockSpec(memory_space=pl.ANY),
             pl.BlockSpec(memory_space=pltpu.VMEM),
         ),
         scratch_shapes=[
+            pltpu.SMEM(plan_lengths.shape, jnp.int32),
+            pltpu.SMEM(shard_of_class.shape, jnp.int32),
+            pltpu.VMEM((bal, vloc), bf),
             pltpu.VMEM((feat, vloc), bf),
+            pltpu.VMEM((chunks, CBLK, vloc), bf),
             pltpu.VMEM((steps, slots, KBLK), bf),
             pltpu.VMEM((slots, vloc), f32),
             pltpu.VMEM((slots, vloc), f32),
@@ -408,11 +444,11 @@
             pltpu.VMEM((GROUPS, n, dep, vloc), bf),
             pltpu.VMEM((GROUPS, nv, 8, rows), f32),
             pltpu.VMEM((n, 8, slots), f32),
-            pltpu.VMEM((GROUPS, chunks, rows, CBLK), f32),
-            pltpu.VMEM((GROUPS, chunks, rows, CBLK), f32),
+            pltpu.VMEM((slots, vloc), bf),
             pltpu.VMEM((GROUPS, chunks, rows, CBLK), bf),
             pltpu.VMEM((GROUPS, chunks, rows, CBLK), bf),
             pltpu.VMEM((GROUPS, chunks, rows, CBLK), bf),
+            dma((3,)),
             dma((steps,)),
             dma((steps,)),
             dma((GROUPS, n)),
@@ -422,8 +458,10 @@
             dma((GROUPS, nv)),
             dma((n,)),
             dma((n,)),
-            dma((GROUPS, chunks)),
-            dma((GROUPS, chunks)),
+            dma((chunks,)),
+            dma((chunks,)),
+            dma((GROUPS,)),
+            dma((GROUPS,)),
             dma((GROUPS, chunks)),
             dma((GROUPS, chunks)),
             dma((GROUPS, chunks)),

time: 61.2 us -> 59.9 us (0.979)
  Pallas kernels: 56.1 us -> 54.9 us
    pallas_call x1, Pallas kernels: 56.1 us -> 54.9 us  [body(): pl.pallas_call(functools.partial(kernel, n, nv), out_shape=(jax.ShapeDtyp...]
where the time goes in v2:
time: 59.9 us; the launch traced here: 59.7 us
  Pallas kernels  54.9 us (92%)
  local copies, waits for them, and re-layouts  4.23 us (7%)
  between operations  0.65 us (1%)
    pallas_call x1, Pallas kernels, body(): pl.pallas_call(functools.partial(kernel, n, nv), out_shape=(jax.ShapeDtyp...  54.9 us
    unnamed x8, local copies, waits for them, and re-layouts  4.23 us

profile of v2, /device:TPU:29, one launch (start us, length us, event | category | flops | bytes accessed | tf_op | source)
XLA Modules:
  0.0 59.7 jit_solution(8735909786754062664)
XLA Ops:
  0.6 0.0 copy-start
  0.6 0.9 %copy-done = bf16[128,768]{1,0:T(8,128)(2,1)S(1)} copy-done((bf16[128,768]{1,0:T(8,128)(2,1)S(1)}, bf16[128,768]{1,0:T(8,128)(2,1)}, u32[]{:S(2)}) %copy-start) | copy-done | bytes 196632
  1.6 0.0 copy-start.1
  1.6 0.7 %copy-done.1 = s32[8]{0:T(128)S(1)} copy-done((s32[8]{0:T(128)S(1)}, s32[8]{0:T(128)}, u32[]{:S(2)}) %copy-start.1) | copy-done | bytes 56
  2.2 0.0 copy-start.2
  2.2 0.7 %copy-done.2 = s32[8]{0:T(128)S(1)} copy-done((s32[8]{0:T(128)S(1)}, s32[8]{0:T(128)}, u32[]{:S(2)}) %copy-start.2) | copy-done | bytes 56
  2.9 54.9 %plan_loss.1 = (bf16[256,5120]{1,0:T(8,128)(2,1)S(1)}, f32[1,128]{1,0:T(1,128)S(1)}) custom-call(s32[8]{0:T(128)S(1)} %copy-done.1, s32[8]{0:T(128)S(1)} %copy-done.2, bf16[128,768]{1,0:T(8,128)(2,1)S(1)} %copy-done, bf16[256,5120]{1,0:T(8,128)(2,1)} %hid_hbm.1, bf16[5120,768]{1,0:T(8,128)(2,1)} %w_hbm.1), custom_call_target="tpu_custom_call" | custom-call | flops 4026531840 | bytes 13107200 | tf_op jit(solution)/shard_map/plan_loss/pallas_call | solution.py:416
  57.7 1.5 %copy.9 = bf16[256,5120]{1,0:T(8,128)(2,1)} copy(bf16[256,5120]{1,0:T(8,128)(2,1)S(1)} %get-tuple-element.8) | data formatting | bytes 5242880
  59.2 0.5 copy.10
Async XLA Ops:
  0.6 0.9 %copy-start = (bf16[128,768]{1,0:T(8,128)(2,1)S(1)}, bf16[128,768]{1,0:T(8,128)(2,1)}, u32[]{:S(2)}) copy-start(bf16[128,768]{1,0:T(8,128)(2,1)} %teach_hbm.1) | copy-start | bytes 589828
  1.6 0.7 %copy-start.1 = (s32[8]{0:T(128)S(1)}, s32[8]{0:T(128)}, u32[]{:S(2)}) copy-start(s32[8]{0:T(128)} %len_hbm.1) | copy-start | bytes 100
  2.2 0.7 %copy-start.2 = (s32[8]{0:T(128)S(1)}, s32[8]{0:T(128)}, u32[]{:S(2)}) copy-start(s32[8]{0:T(128)} %soc_hbm.1) | copy-start | bytes 100

commit v3 on v2

--- a/solution.py
+++ b/solution.py
@@ -11,7 +11,7 @@
 MESH = pl.DeviceIdType.MESH
 GROUPS = 2
 KBLK = 512
-CBLK = 512
+CBLK = 256
 
 
 def kernel(
@@ -124,16 +124,21 @@
         off_me = off_me + jnp.where(me == s, offs[s], zero)
         len_me = len_me + jnp.where(me == s, lens[s], zero)
 
+    line = lax.broadcasted_iota(jnp.int32, (n * dep, 1), 0)
+    first = jnp.zeros((n * dep, 1), jnp.int32)
+    for s in range(n):
+        b0 = lax.shift_right_logical(offs[s] + ((inv_me - offs[s]) & (n - 1)), shift)
+        inside = (line >= s * dep) & (line < (s + 1) * dep)
+        first = jnp.where(inside, b0 - s * dep, first)
+    target = line + first
+    b = lax.broadcasted_iota(jnp.int32, (n * dep, bal), 1)
     for g in range(GROUPS):
-        for s in range(n):
-            b0 = lax.shift_right_logical(offs[s] + ((inv_me - offs[s]) & (n - 1)), shift)
-            first = b0 + g * per
-            r = lax.broadcasted_iota(jnp.int32, (dep, bal), 0)
-            b = lax.broadcasted_iota(jnp.int32, (dep, bal), 1)
-            hot = jnp.where(b == r + first, 1.0, 0.0).astype(jnp.bfloat16)
-            tout[g, s] = jnp.dot(
-                hot, teach_ref[...], preferred_element_type=jnp.float32
-            ).astype(jnp.bfloat16)
+        hot = jnp.where(b == target + g * per, 1.0, 0.0).astype(jnp.bfloat16)
+        tout[g] = (
+            jnp.dot(hot, teach_ref[...], preferred_element_type=jnp.float32)
+            .astype(jnp.bfloat16)
+            .reshape(n, dep, vloc)
+        )
 
     def t_send(g, to):
         return pltpu.make_async_remote_copy(

time: 59.9 us -> 59.8 us (level)
  no operation moved by 1% of the time
where the time goes in v3:
time: 59.8 us; the launch traced here: 59.7 us
  Pallas kernels  54.8 us (92%)
  local copies, waits for them, and re-layouts  4.23 us (7%)
  between operations  0.65 us (1%)
    pallas_call x1, Pallas kernels, body(): pl.pallas_call(functools.partial(kernel, n, nv), out_shape=(jax.ShapeDtyp...  54.8 us
    unnamed x8, local copies, waits for them, and re-layouts  4.23 us

profile of v3, /device:TPU:29, one launch (start us, length us, event | category | flops | bytes accessed | tf_op | source)
XLA Modules:
  0.0 59.7 jit_solution(7300041162692246153)
XLA Ops:
  0.6 0.0 copy-start
  0.6 0.9 %copy-done = bf16[128,768]{1,0:T(8,128)(2,1)S(1)} copy-done((bf16[128,768]{1,0:T(8,128)(2,1)S(1)}, bf16[128,768]{1,0:T(8,128)(2,1)}, u32[]{:S(2)}) %copy-start) | copy-done | bytes 196632
  1.6 0.0 copy-start.1
  1.6 0.7 %copy-done.1 = s32[8]{0:T(128)S(1)} copy-done((s32[8]{0:T(128)S(1)}, s32[8]{0:T(128)}, u32[]{:S(2)}) %copy-start.1) | copy-done | bytes 56
  2.2 0.0 copy-start.2
  2.2 0.7 %copy-done.2 = s32[8]{0:T(128)S(1)} copy-done((s32[8]{0:T(128)S(1)}, s32[8]{0:T(128)}, u32[]{:S(2)}) %copy-start.2) | copy-done | bytes 56
  2.9 54.8 %plan_loss.1 = (bf16[256,5120]{1,0:T(8,128)(2,1)S(1)}, f32[1,128]{1,0:T(1,128)S(1)}) custom-call(s32[8]{0:T(128)S(1)} %copy-done.1, s32[8]{0:T(128)S(1)} %copy-done.2, bf16[128,768]{1,0:T(8,128)(2,1)S(1)} %copy-done, bf16[256,5120]{1,0:T(8,128)(2,1)} %hid_hbm.1, bf16[5120,768]{1,0:T(8,128)(2,1)} %w_hbm.1), custom_call_target="tpu_custom_call" | custom-call | flops 4026531840 | bytes 13107200 | tf_op jit(solution)/shard_map/plan_loss/pallas_call | solution.py:421
  57.7 1.5 %copy.9 = bf16[256,5120]{1,0:T(8,128)(2,1)} copy(bf16[256,5120]{1,0:T(8,128)(2,1)S(1)} %get-tuple-element.8) | data formatting | bytes 5242880
  59.2 0.5 copy.10
Async XLA Ops:
  0.6 0.9 %copy-start = (bf16[128,768]{1,0:T(8,128)(2,1)S(1)}, bf16[128,768]{1,0:T(8,128)(2,1)}, u32[]{:S(2)}) copy-start(bf16[128,768]{1,0:T(8,128)(2,1)} %teach_hbm.1) | copy-start | bytes 589828
  1.6 0.7 %copy-start.1 = (s32[8]{0:T(128)S(1)}, s32[8]{0:T(128)}, u32[]{:S(2)}) copy-start(s32[8]{0:T(128)} %len_hbm.1) | copy-start | bytes 100
  2.2 0.7 %copy-start.2 = (s32[8]{0:T(128)S(1)}, s32[8]{0:T(128)}, u32[]{:S(2)}) copy-start(s32[8]{0:T(128)} %soc_hbm.1) | copy-start | bytes 100

commit v4 on v3

--- a/solution.py
+++ b/solution.py
@@ -11,7 +11,7 @@
 MESH = pl.DeviceIdType.MESH
 GROUPS = 2
 KBLK = 512
-CBLK = 256
+CBLK = 512
 
 
 def kernel(
@@ -212,8 +212,8 @@
 
     def g_copy(g):
         return pltpu.make_async_remote_copy(
-            src_ref=g_v.at[pl.ds(g * rows, rows), :],
-            dst_ref=g_sib.at[pl.ds(g * rows, rows), :],
+            src_ref=g_v.at[g],
+            dst_ref=g_sib.at[g],
             send_sem=gs_sem.at[g],
             recv_sem=gr_sem.at[g],
             device_id=(me, sib),
@@ -257,10 +257,8 @@
     def f_own(g, j):
         return pltpu.make_async_copy(fin.at[g, j], place(g, core, j), fl_sem.at[g, j])
 
-    def back(grad, weight):
-        return lax.dot_general(
-            grad, weight, (((1,), (1,)), ((), ())), preferred_element_type=jnp.float32
-        )
+    def back(weight, grad):
+        return jnp.dot(weight, grad, preferred_element_type=jnp.float32)
 
     for g in range(GROUPS):
         span = pl.ds(g * rows, rows)
@@ -324,7 +322,7 @@
         mass_c = back_cols[:, 1:2]
         z = jnp.where(live, z_v[span, :], 0.0)
         grad = loss_scale * (mass_c * jnp.exp(z - lse_c) - q_v[span, :])
-        g_v[span, :] = jnp.where(live, grad, 0.0).astype(jnp.bfloat16)
+        g_v[g] = jnp.where(live, grad, 0.0).T.astype(jnp.bfloat16)
 
         g_copy(g).start()
         g_copy(g).wait_recv()
@@ -334,7 +332,7 @@
             if g == 0:
                 w_push(j).wait_recv()
             own = w_v[pl.ds(pl.multiple_of(core * half + j * CBLK, CBLK), CBLK), :]
-            mine = back(g_v[span, :], own) + back(g_sib[span, :], w_sib[j])
+            mine = back(own, g_v[g]) + back(w_sib[j], g_sib[g])
             xs[g, j] = mine.astype(jnp.bfloat16)
             x_copy(g, j).start()
 
@@ -374,9 +372,8 @@
         @pl.loop(0, chunks)
         def _(j):
             x_copy(g, j).wait_recv()
-            fin[g, j] = (xs[g, j].astype(jnp.float32) + xr[g, j].astype(jnp.float32)).astype(
-                jnp.bfloat16
-            )
+            both = xs[g, j].astype(jnp.float32) + xr[g, j].astype(jnp.float32)
+            fin[g, j] = both.T.astype(jnp.bfloat16)
             f_send(g, j).start()
             f_own(g, j).start()
 
@@ -444,14 +441,14 @@
             pltpu.VMEM((steps, slots, KBLK), bf),
             pltpu.VMEM((slots, vloc), f32),
             pltpu.VMEM((slots, vloc), f32),
-            pltpu.VMEM((slots, vloc), bf),
+            pltpu.VMEM((GROUPS, vloc, rows), bf),
             pltpu.VMEM((GROUPS, n, dep, vloc), bf),
             pltpu.VMEM((GROUPS, n, dep, vloc), bf),
             pltpu.VMEM((GROUPS, nv, 8, rows), f32),
             pltpu.VMEM((n, 8, slots), f32),
-            pltpu.VMEM((slots, vloc), bf),
-            pltpu.VMEM((GROUPS, chunks, rows, CBLK), bf),
-            pltpu.VMEM((GROUPS, chunks, rows, CBLK), bf),
+            pltpu.VMEM((GROUPS, vloc, rows), bf),
+            pltpu.VMEM((GROUPS, chunks, CBLK, rows), bf),
+            pltpu.VMEM((GROUPS, chunks, CBLK, rows), bf),
             pltpu.VMEM((GROUPS, chunks, rows, CBLK), bf),
             dma((3,)),
             dma((steps,)),

time: 59.8 us -> 60 us (level)
  no operation moved by 1% of the time
where the time goes in v4:
time: 60 us; the launch traced here: 59.9 us
  Pallas kernels  55 us (92%)
  local copies, waits for them, and re-layouts  4.23 us (7%)
  between operations  0.65 us (1%)
    pallas_call x1, Pallas kernels, body(): pl.pallas_call(functools.partial(kernel, n, nv), out_shape=(jax.ShapeDtyp...  55 us
    unnamed x8, local copies, waits for them, and re-layouts  4.23 us

profile of v4, /device:TPU:29, one launch (start us, length us, event | category | flops | bytes accessed | tf_op | source)
XLA Modules:
  0.0 59.9 jit_solution(106939623370628043)
XLA Ops:
  0.6 0.0 copy-start
  0.6 0.9 %copy-done = bf16[128,768]{1,0:T(8,128)(2,1)S(1)} copy-done((bf16[128,768]{1,0:T(8,128)(2,1)S(1)}, bf16[128,768]{1,0:T(8,128)(2,1)}, u32[]{:S(2)}) %copy-start) | copy-done | bytes 196632
  1.6 0.0 copy-start.1
  1.6 0.7 %copy-done.1 = s32[8]{0:T(128)S(1)} copy-done((s32[8]{0:T(128)S(1)}, s32[8]{0:T(128)}, u32[]{:S(2)}) %copy-start.1) | copy-done | bytes 56
  2.2 0.0 copy-start.2
  2.2 0.7 %copy-done.2 = s32[8]{0:T(128)S(1)} copy-done((s32[8]{0:T(128)S(1)}, s32[8]{0:T(128)}, u32[]{:S(2)}) %copy-start.2) | copy-done | bytes 56
  2.9 55.0 %plan_loss.1 = (bf16[256,5120]{1,0:T(8,128)(2,1)S(1)}, f32[1,128]{1,0:T(1,128)S(1)}) custom-call(s32[8]{0:T(128)S(1)} %copy-done.1, s32[8]{0:T(128)S(1)} %copy-done.2, bf16[128,768]{1,0:T(8,128)(2,1)S(1)} %copy-done, bf16[256,5120]{1,0:T(8,128)(2,1)} %hid_hbm.1, bf16[5120,768]{1,0:T(8,128)(2,1)} %w_hbm.1), custom_call_target="tpu_custom_call" | custom-call | flops 4026531840 | bytes 13107200 | tf_op jit(solution)/shard_map/plan_loss/pallas_call | solution.py:418
  57.8 1.5 %copy.9 = bf16[256,5120]{1,0:T(8,128)(2,1)} copy(bf16[256,5120]{1,0:T(8,128)(2,1)S(1)} %get-tuple-element.8) | data formatting | bytes 5242880
  59.3 0.5 copy.10
Async XLA Ops:
  0.6 0.9 %copy-start = (bf16[128,768]{1,0:T(8,128)(2,1)S(1)}, bf16[128,768]{1,0:T(8,128)(2,1)}, u32[]{:S(2)}) copy-start(bf16[128,768]{1,0:T(8,128)(2,1)} %teach_hbm.1) | copy-start | bytes 589828
  1.6 0.7 %copy-start.1 = (s32[8]{0:T(128)S(1)}, s32[8]{0:T(128)}, u32[]{:S(2)}) copy-start(s32[8]{0:T(128)} %len_hbm.1) | copy-start | bytes 100
  2.2 0.7 %copy-start.2 = (s32[8]{0:T(128)S(1)}, s32[8]{0:T(128)}, u32[]{:S(2)}) copy-start(s32[8]{0:T(128)} %soc_hbm.1) | copy-start | bytes 100

commit v5 on v4

--- a/solution.py
+++ b/solution.py
@@ -182,23 +182,9 @@
             def _(j):
                 w_push(j).start()
 
+        for k in sorted(range(1, n), key=lambda k: abs(2 * k - n)):
+            t_send(g, lax.rem(me + k, n)).start()
         t_own(g).start()
-
-        @pl.loop(1, n)
-        def _(k):
-            t_send(g, lax.rem(me + k, n)).start()
-
-    z_v[...] = jnp.zeros_like(z_v)
-
-    @pl.loop(0, steps)
-    def _(k):
-        w_load(k).wait()
-        h_load(k).wait()
-        z_v[...] += jnp.dot(
-            h_v[k],
-            w_v[pl.ds(pl.multiple_of(k * KBLK, KBLK), KBLK), :],
-            preferred_element_type=jnp.float32,
-        )
 
     def s_copy(g, frm, to):
         return pltpu.make_async_remote_copy(
@@ -262,6 +248,19 @@
 
     for g in range(GROUPS):
         span = pl.ds(g * rows, rows)
+        z_v[span, :] = jnp.zeros((rows, vloc), jnp.float32)
+
+        @pl.loop(0, steps)
+        def _(k):
+            if g == 0:
+                w_load(k).wait()
+                h_load(k).wait()
+            z_v[span, :] += jnp.dot(
+                h_v[k, span, :],
+                w_v[pl.ds(pl.multiple_of(k * KBLK, KBLK), KBLK), :],
+                preferred_element_type=jnp.float32,
+            )
+
         slot = lax.broadcasted_iota(jnp.int32, (rows, 1), 0) + g * rows
         live = slot < len_me
         cls = (off_me + slot) & (n - 1)
@@ -350,6 +349,18 @@
     def _(k):
         k_copy(me, lax.rem(me + k, n)).start()
 
+    def finish(g):
+        @pl.loop(0, chunks)
+        def _(j):
+            x_copy(g, j).wait_recv()
+            both = xs[g, j].astype(jnp.float32) + xr[g, j].astype(jnp.float32)
+            fin[g, j] = both.T.astype(jnp.bfloat16)
+            f_send(g, j).start()
+            f_own(g, j).start()
+
+    for g in range(GROUPS - 1):
+        finish(g)
+
     @pl.loop(1, n)
     def _(k):
         frm = lax.rem(me + k, n)
@@ -367,15 +378,7 @@
     )
     kl_ref[...] = jnp.sum(jnp.where(diag, kl_col, 0.0), axis=0, keepdims=True)
 
-    for g in range(GROUPS):
-
-        @pl.loop(0, chunks)
-        def _(j):
-            x_copy(g, j).wait_recv()
-            both = xs[g, j].astype(jnp.float32) + xr[g, j].astype(jnp.float32)
-            fin[g, j] = both.T.astype(jnp.bfloat16)
-            f_send(g, j).start()
-            f_own(g, j).start()
+    finish(GROUPS - 1)
 
     for g in range(GROUPS):
 

time: 60 us -> 60.1 us (level)
  the two profiles are of different devices: /device:TPU:29 before, /device:TPU:17 now
where the time goes in v5:
time: 60.1 us; the launch traced here: 60 us
  Pallas kernels  55.1 us (92%)
  local copies, waits for them, and re-layouts  4.23 us (7%)
  between operations  0.65 us (1%)
    pallas_call x1, Pallas kernels, body(): pl.pallas_call(functools.partial(kernel, n, nv), out_shape=(jax.ShapeDtyp...  55.1 us
    unnamed x8, local copies, waits for them, and re-layouts  4.23 us

profile of v5, /device:TPU:17, one launch (start us, length us, event | category | flops | bytes accessed | tf_op | source)
XLA Modules:
  0.0 60.0 jit_solution(14682170705494169561)
XLA Ops:
  0.6 0.0 copy-start
  0.6 0.9 %copy-done = bf16[128,768]{1,0:T(8,128)(2,1)S(1)} copy-done((bf16[128,768]{1,0:T(8,128)(2,1)S(1)}, bf16[128,768]{1,0:T(8,128)(2,1)}, u32[]{:S(2)}) %copy-start) | copy-done | bytes 196632
  1.6 0.0 copy-start.1
  1.6 0.7 %copy-done.1 = s32[8]{0:T(128)S(1)} copy-done((s32[8]{0:T(128)S(1)}, s32[8]{0:T(128)}, u32[]{:S(2)}) %copy-start.1) | copy-done | bytes 56
  2.2 0.0 copy-start.2
  2.2 0.7 %copy-done.2 = s32[8]{0:T(128)S(1)} copy-done((s32[8]{0:T(128)S(1)}, s32[8]{0:T(128)}, u32[]{:S(2)}) %copy-start.2) | copy-done | bytes 56
  2.9 55.1 %plan_loss.1 = (bf16[256,5120]{1,0:T(8,128)(2,1)S(1)}, f32[1,128]{1,0:T(1,128)S(1)}) custom-call(s32[8]{0:T(128)S(1)} %copy-done.1, s32[8]{0:T(128)S(1)} %copy-done.2, bf16[128,768]{1,0:T(8,128)(2,1)S(1)} %copy-done, bf16[256,5120]{1,0:T(8,128)(2,1)} %hid_hbm.1, bf16[5120,768]{1,0:T(8,128)(2,1)} %w_hbm.1), custom_call_target="tpu_custom_call" | custom-call | flops 4026531840 | bytes 13107200 | tf_op jit(solution)/shard_map/plan_loss/pallas_call | solution.py:421
  58.0 1.5 %copy.9 = bf16[256,5120]{1,0:T(8,128)(2,1)} copy(bf16[256,5120]{1,0:T(8,128)(2,1)S(1)} %get-tuple-element.8) | data formatting | bytes 5242880
  59.5 0.5 copy.10
Async XLA Ops:
  0.6 0.9 %copy-start = (bf16[128,768]{1,0:T(8,128)(2,1)S(1)}, bf16[128,768]{1,0:T(8,128)(2,1)}, u32[]{:S(2)}) copy-start(bf16[128,768]{1,0:T(8,128)(2,1)} %teach_hbm.1) | copy-start | bytes 589828
  1.6 0.7 %copy-start.1 = (s32[8]{0:T(128)S(1)}, s32[8]{0:T(128)}, u32[]{:S(2)}) copy-start(s32[8]{0:T(128)} %len_hbm.1) | copy-start | bytes 100
  2.2 0.7 %copy-start.2 = (s32[8]{0:T(128)S(1)}, s32[8]{0:T(128)}, u32[]{:S(2)}) copy-start(s32[8]{0:T(128)} %soc_hbm.1) | copy-start | bytes 100

commit v6 on v5

--- a/solution.py
+++ b/solution.py
@@ -9,9 +9,9 @@
 
 loss_scale = 64.0
 MESH = pl.DeviceIdType.MESH
-GROUPS = 2
+GROUPS = 1
 KBLK = 512
-CBLK = 512
+CBLK = 256
 
 
 def kernel(
@@ -176,15 +176,14 @@
 
     pl.semaphore_wait(barrier, n - 1 + nv - 1)
     for g in range(GROUPS):
-        if g == 1:
+        for k in sorted(range(1, n), key=lambda k: abs(2 * k - n)):
+            t_send(g, lax.rem(me + k, n)).start()
+        t_own(g).start()
+        if g == 0:
 
             @pl.loop(0, chunks)
             def _(j):
                 w_push(j).start()
-
-        for k in sorted(range(1, n), key=lambda k: abs(2 * k - n)):
-            t_send(g, lax.rem(me + k, n)).start()
-        t_own(g).start()
 
     def s_copy(g, frm, to):
         return pltpu.make_async_remote_copy(

time: 60.1 us -> 58.2 us (0.968)
  the two profiles are of different devices: /device:TPU:17 before, /device:TPU:0 now
where the time goes in v6:
time: 58.2 us; the launch traced here: 58 us
  Pallas kernels  53.2 us (91%)
  local copies, waits for them, and re-layouts  4.23 us (7%)
  between operations  0.65 us (1%)
    pallas_call x1, Pallas kernels, body(): pl.pallas_call(functools.partial(kernel, n, nv), out_shape=(jax.ShapeDtyp...  53.2 us
    unnamed x8, local copies, waits for them, and re-layouts  4.23 us

profile of v6, /device:TPU:0, one launch (start us, length us, event | category | flops | bytes accessed | tf_op | source)
XLA Modules:
  0.0 58.0 jit_solution(4114160852461724929)
XLA Ops:
  0.6 0.0 copy-start
  0.6 0.9 %copy-done = bf16[128,768]{1,0:T(8,128)(2,1)S(1)} copy-done((bf16[128,768]{1,0:T(8,128)(2,1)S(1)}, bf16[128,768]{1,0:T(8,128)(2,1)}, u32[]{:S(2)}) %copy-start) | copy-done | bytes 196632
  1.6 0.0 copy-start.1
  1.6 0.7 %copy-done.1 = s32[8]{0:T(128)S(1)} copy-done((s32[8]{0:T(128)S(1)}, s32[8]{0:T(128)}, u32[]{:S(2)}) %copy-start.1) | copy-done | bytes 56
  2.2 0.0 copy-start.2
  2.2 0.7 %copy-done.2 = s32[8]{0:T(128)S(1)} copy-done((s32[8]{0:T(128)S(1)}, s32[8]{0:T(128)}, u32[]{:S(2)}) %copy-start.2) | copy-done | bytes 56
  2.9 53.2 %plan_loss.1 = (bf16[256,5120]{1,0:T(8,128)(2,1)S(1)}, f32[1,128]{1,0:T(1,128)S(1)}) custom-call(s32[8]{0:T(128)S(1)} %copy-done.1, s32[8]{0:T(128)S(1)} %copy-done.2, bf16[128,768]{1,0:T(8,128)(2,1)S(1)} %copy-done, bf16[256,5120]{1,0:T(8,128)(2,1)} %hid_hbm.1, bf16[5120,768]{1,0:T(8,128)(2,1)} %w_hbm.1), custom_call_target="tpu_custom_call" | custom-call | flops 4026531840 | bytes 13107200 | tf_op jit(solution)/shard_map/plan_loss/pallas_call | solution.py:420
  56.0 1.5 %copy.9 = bf16[256,5120]{1,0:T(8,128)(2,1)} copy(bf16[256,5120]{1,0:T(8,128)(2,1)S(1)} %get-tuple-element.8) | data formatting | bytes 5242880
  57.5 0.5 copy.10
Async XLA Ops:
  0.6 0.9 %copy-start = (bf16[128,768]{1,0:T(8,128)(2,1)S(1)}, bf16[128,768]{1,0:T(8,128)(2,1)}, u32[]{:S(2)}) copy-start(bf16[128,768]{1,0:T(8,128)(2,1)} %teach_hbm.1) | copy-start | bytes 589828
  1.6 0.7 %copy-start.1 = (s32[8]{0:T(128)S(1)}, s32[8]{0:T(128)}, u32[]{:S(2)}) copy-start(s32[8]{0:T(128)} %len_hbm.1) | copy-start | bytes 100
  2.2 0.7 %copy-start.2 = (s32[8]{0:T(128)S(1)}, s32[8]{0:T(128)}, u32[]{:S(2)}) copy-start(s32[8]{0:T(128)} %soc_hbm.1) | copy-start | bytes 100

commit v7 on v6

--- a/solution.py
+++ b/solution.py
@@ -357,7 +357,7 @@
             f_send(g, j).start()
             f_own(g, j).start()
 
-    for g in range(GROUPS - 1):
+    for g in range(GROUPS):
         finish(g)
 
     @pl.loop(1, n)
@@ -376,8 +376,6 @@
         jnp.int32, (bal, bal), 1
     )
     kl_ref[...] = jnp.sum(jnp.where(diag, kl_col, 0.0), axis=0, keepdims=True)
-
-    finish(GROUPS - 1)
 
     for g in range(GROUPS):
 

time: 58.2 us -> 58.2 us (level)
  no operation moved by 1% of the time
where the time goes in v7:
time: 58.2 us; the launch traced here: 58 us
  Pallas kernels  53.2 us (91%)
  local copies, waits for them, and re-layouts  4.23 us (7%)
  between operations  0.65 us (1%)
    pallas_call x1, Pallas kernels, body(): pl.pallas_call(functools.partial(kernel, n, nv), out_shape=(jax.ShapeDtyp...  53.2 us
    unnamed x8, local copies, waits for them, and re-layouts  4.23 us

profile of v7, /device:TPU:0, one launch (start us, length us, event | category | flops | bytes accessed | tf_op | source)
XLA Modules:
  0.0 58.0 jit_solution(10793431850012764183)
XLA Ops:
  0.6 0.0 copy-start
  0.6 0.9 %copy-done = bf16[128,768]{1,0:T(8,128)(2,1)S(1)} copy-done((bf16[128,768]{1,0:T(8,128)(2,1)S(1)}, bf16[128,768]{1,0:T(8,128)(2,1)}, u32[]{:S(2)}) %copy-start) | copy-done | bytes 196632
  1.6 0.0 copy-start.1
  1.6 0.7 %copy-done.1 = s32[8]{0:T(128)S(1)} copy-done((s32[8]{0:T(128)S(1)}, s32[8]{0:T(128)}, u32[]{:S(2)}) %copy-start.1) | copy-done | bytes 56
  2.2 0.0 copy-start.2
  2.2 0.7 %copy-done.2 = s32[8]{0:T(128)S(1)} copy-done((s32[8]{0:T(128)S(1)}, s32[8]{0:T(128)}, u32[]{:S(2)}) %copy-start.2) | copy-done | bytes 56
  2.9 53.2 %plan_loss.1 = (bf16[256,5120]{1,0:T(8,128)(2,1)S(1)}, f32[1,128]{1,0:T(1,128)S(1)}) custom-call(s32[8]{0:T(128)S(1)} %copy-done.1, s32[8]{0:T(128)S(1)} %copy-done.2, bf16[128,768]{1,0:T(8,128)(2,1)S(1)} %copy-done, bf16[256,5120]{1,0:T(8,128)(2,1)} %hid_hbm.1, bf16[5120,768]{1,0:T(8,128)(2,1)} %w_hbm.1), custom_call_target="tpu_custom_call" | custom-call | flops 4026531840 | bytes 13107200 | tf_op jit(solution)/shard_map/plan_loss/pallas_call | solution.py:418
  56.0 1.5 %copy.9 = bf16[256,5120]{1,0:T(8,128)(2,1)} copy(bf16[256,5120]{1,0:T(8,128)(2,1)S(1)} %get-tuple-element.8) | data formatting | bytes 5242880
  57.5 0.5 copy.10
Async XLA Ops:
  0.6 0.9 %copy-start = (bf16[128,768]{1,0:T(8,128)(2,1)S(1)}, bf16[128,768]{1,0:T(8,128)(2,1)}, u32[]{:S(2)}) copy-start(bf16[128,768]{1,0:T(8,128)(2,1)} %teach_hbm.1) | copy-start | bytes 589828
  1.6 0.7 %copy-start.1 = (s32[8]{0:T(128)S(1)}, s32[8]{0:T(128)}, u32[]{:S(2)}) copy-start(s32[8]{0:T(128)} %len_hbm.1) | copy-start | bytes 100
  2.2 0.7 %copy-start.2 = (s32[8]{0:T(128)S(1)}, s32[8]{0:T(128)}, u32[]{:S(2)}) copy-start(s32[8]{0:T(128)} %soc_hbm.1) | copy-start | bytes 100
